TPU v7x, 1024 devices: a whole 4x4x32 slice. The times are simulated.
1024 devices in a mesh: row: 32 (over z_lo, y), col: 32 (over z_hi, x, core).
Axes of the slice: x: 4, y: 4, z: 32 (z_hi: 4, z_lo: 8; z = z_hi * 8 + z_lo), core: 2. Of those that a mesh axis runs over, the one named last changes fastest.
Arguments:
- features: bfloat16 [131072, 256], P(('col', 'row')), may hold values from -6 to 6
- tile_values: bfloat16 [32, 32, 24, 128, 128], P('row', 'col'), may hold values from 0.0049743652 to 0.099609375
- tile_rows: int32 [32, 32, 24], P('row', 'col'), may hold values from 0 to 31
- tile_cols: int32 [32, 32, 24], P('row', 'col'), may hold values from 0 to 31
- tile_count: int32 [32, 32], P('row', 'col'), may hold values from 6 to 24, as said below
- weight: bfloat16 [256, 256], replicated, may hold values from -0.375 to 0.375
- out_grad: bfloat16 [131072, 256], P(('row', 'col')), may hold values from -6 to 6
Outputs:
- layer_out: bfloat16 [131072, 256], P(('row', 'col'))
- grad_x: bfloat16 [131072, 256], P(('col', 'row'))
Inputs may be any that keep to these rules, and one draw needn't show every extreme that they name: `tile_count`: live tile slots of a block; some block has all 24 slots live.
All inputs are finite; a program needn't handle non-finite values.
Results may differ from a plain program's by a relative error of at most 0.03.
Values may be sent and summed in bfloat16 or wider, within the bound.
A program may use at most 32 MiB of HBM per device.

v0:
```python
import jax
import jax.numpy as jnp
from jax import lax
from jax.sharding import PartitionSpec as P

TILE = 128


def activate(value):
    inner = 0.7978845608 * (value + 0.044715 * value * value * value)
    return 0.5 * value * (1.0 + jnp.tanh(inner))


def place_tiles(products, indices, count_tiles):
    slots, tile_len, width = products.shape
    placed = jnp.zeros((count_tiles, tile_len, width), jnp.float32).at[indices].add(products)
    return placed.reshape(count_tiles * tile_len, width)


def times_weight_t(left, weight):
    return lax.dot_general(
        left, weight, (((1,), (1,)), ((), ())), preferred_element_type=jnp.float32
    )


def per_device(features, tile_values, tile_rows, tile_cols, tile_count, weight, out_grad):
    source_block = lax.all_gather(features, "row", axis=0, tiled=True)
    block_len, width = source_block.shape
    count_tiles = block_len // TILE
    slot_count = tile_values.shape[2]
    live_mask = jnp.arange(slot_count) < tile_count[0, 0]
    tile_vals = jnp.where(live_mask[:, None, None], tile_values[0, 0], jnp.zeros((), jnp.bfloat16))
    row_index = tile_rows[0, 0]
    col_index = tile_cols[0, 0]
    sources = source_block.reshape(count_tiles, TILE, width)[col_index]
    products = jnp.einsum("kab,kbf->kaf", tile_vals, sources, preferred_element_type=jnp.float32)
    partial_value = place_tiles(products, row_index, count_tiles)
    aggregated = lax.psum_scatter(
        partial_value.astype(jnp.bfloat16), "col", scatter_dimension=0, tiled=True
    )
    preact = jnp.dot(aggregated, weight, preferred_element_type=jnp.float32)
    activated, pullback = jax.vjp(activate, preact)
    layer_out = activated.astype(jnp.bfloat16)
    pre_grad = pullback(out_grad.astype(jnp.float32))[0].astype(jnp.bfloat16)
    projected = times_weight_t(pre_grad, weight).astype(jnp.bfloat16)
    grad_block = lax.all_gather(projected, "col", axis=0, tiled=True)
    grads = grad_block.reshape(count_tiles, TILE, width)[row_index]
    back_products = jnp.einsum("kab,kaf->kbf", tile_vals, grads, preferred_element_type=jnp.float32)
    back_partial = place_tiles(back_products, col_index, count_tiles)
    grad_x = lax.psum_scatter(
        back_partial.astype(jnp.bfloat16), "row", scatter_dimension=0, tiled=True
    )
    return (layer_out, grad_x)


def solution(mesh):
    in_specs = (
        P(("col", "row"), None),
        P("row", "col", None, None, None),
        P("row", "col", None),
        P("row", "col", None),
        P("row", "col"),
        P(),
        P(("row", "col"), None),
    )
    out_specs = (P(("row", "col"), None), P(("col", "row"), None))
    return jax.shard_map(
        per_device, mesh=mesh, in_specs=in_specs, out_specs=out_specs, check_vma=False
    )
```

profile of v0, /device:TPU:6, one launch (start us, length us, event | category | flops | bytes accessed | tf_op | source)
XLA Modules:
  0.0 849.4 jit_solution(17339069253098861422)
XLA Ops:
  7.2 0.0 copy-start
  7.2 0.0 all-gather.3.cloned.1.call-start
  7.2 0.7 all-gather.3.cloned.1.call-update
  7.9 0.0 reduce-scatter.3.cloned.1.call-start
  8.6 0.7 fusion.19
  9.3 0.7 fusion.18
  9.9 242.6 %all-gather.3.cloned.1.call-done = bf16[4096,256]{1,0:T(8,128)(2,1)} async-done(((bf16[128,256]{1,0:T(8,128)(2,1)}), bf16[4096,256]{1,0:T(8,128)(2,1)}) %all-gather.3.cloned.1.call-update) | async-done | bytes 2097168 | tf_op jit(solution)/shard_map/all_gather | solution.py:27
  252.5 3.4 gather_fusion
  255.9 2.3 fusion.1
  258.2 2.4 broadcast.53.clone
  260.7 8.2 scatter_fusion
  268.8 3.8 convert_element_type.24
  272.6 0.0 copy-start.1
  272.6 0.0 reduce-scatter.3.cloned.1.call-update
  272.7 0.0 all-gather.5.cloned.1.call-start
  272.7 180.6 %reduce-scatter.3.cloned.1.call-done = bf16[128,256]{1,0:T(8,128)(2,1)} async-done(((bf16[4096,256]{1,0:T(8,128)(2,1)}), bf16[128,256]{1,0:T(8,128)(2,1)}) %reduce-scatter.3.cloned.1.call-update) | async-done | bytes 65552 | tf_op jit(solution)/shard_map/reduce_scatter | solution.py:38
  453.3 0.0 copy-done
  453.3 1.7 multiply_convert_fusion
  455.0 0.0 copy-done.1
  455.0 0.9 convolution_convert_fusion
  455.9 0.0 all-gather.5.cloned.1.call-update
  455.9 0.0 reduce-scatter.5.cloned.1.call-start
  456.0 123.0 %all-gather.5.cloned.1.call-done = bf16[4096,256]{1,0:T(8,128)(2,1)} async-done(((bf16[128,256]{1,0:T(8,128)(2,1)}), bf16[4096,256]{1,0:T(8,128)(2,1)}) %all-gather.5.cloned.1.call-update) | async-done | bytes 2097168 | tf_op jit(solution)/shard_map/all_gather | solution.py:46
  579.0 3.4 gather_fusion.1
  582.4 2.6 fusion
  585.0 2.4 broadcast.53
  587.4 8.3 scatter_fusion.1
  595.7 3.8 convert_element_type.30
  599.5 0.0 reduce-scatter.5.cloned.1.call-update
  599.5 243.4 %reduce-scatter.5.cloned.1.call-done = bf16[128,256]{1,0:T(8,128)(2,1)} async-done(((bf16[4096,256]{1,0:T(8,128)(2,1)}), bf16[128,256]{1,0:T(8,128)(2,1)}) %reduce-scatter.5.cloned.1.call-update) | async-done | bytes 65552 | tf_op jit(solution)/shard_map/reduce_scatter | solution.py:50
  (3 shorter events, 0.0 us)
Async XLA Ops:
  7.2 446.2 %copy-start = (bf16[256,256]{1,0:T(8,128)(2,1)S(1)}, bf16[256,256]{1,0:T(8,128)(2,1)}, u32[]{:S(2)}) copy-start(bf16[256,256]{1,0:T(8,128)(2,1)} %param.12) | copy-start | bytes 393220
  7.2 245.3 %all-gather.3.cloned.1.call-start = ((), (), s32[]{:S(2)}) async-start(), calls=%async_computation.2 | async-start | bytes 2162688 | tf_op jit(solution)/shard_map/all_gather | solution.py:27
  7.9 445.4 %reduce-scatter.3.cloned.1.call-start = ((), (), s32[]{:S(2)}) async-start(), calls=%async_computation.3 | async-start | bytes 2162688 | tf_op jit(solution)/shard_map/reduce_scatter | solution.py:38
  272.6 182.4 %copy-start.1 = (bf16[128,256]{1,0:T(8,128)(2,1)S(1)}, bf16[128,256]{1,0:T(8,128)(2,1)}, u32[]{:S(2)}) copy-start(bf16[128,256]{1,0:T(8,128)(2,1)} %param.13) | copy-start | bytes 196612
  272.7 306.3 %all-gather.5.cloned.1.call-start = ((), (), s32[]{:S(2)}) async-start(), calls=%async_computation.4 | async-start | bytes 2162688 | tf_op jit(solution)/shard_map/all_gather | solution.py:46
  455.9 387.0 %reduce-scatter.5.cloned.1.call-start = ((), (), s32[]{:S(2)}) async-start(), calls=%async_computation.5 | async-start | bytes 2162688 | tf_op jit(solution)/shard_map/reduce_scatter | solution.py:50
Sparse Core Ops, SparseCore 0:
  10.7 241.7 all-gather.2
  272.8 180.4 reduce-scatter.2
  458.2 120.7 all-gather.4
  599.6 243.2 reduce-scatter.4
where the time goes:
time: 850 us; the launch traced here: 849 us
  waiting for transfers between devices  790 us (93%)
  other arithmetic  25.4 us (3%)
  between operations  14.4 us (2%)
  local copies, waits for them, and re-layouts  11.7 us (1%)
    reduce_scatter x1, waiting for transfers between devices, per_device(): lax.psum_scatter(back_partial.astype(jnp.bfloat16), 'row', scatter_dimens...  243 us
    all_gather x1, waiting for transfers between devices, per_device(): source_block = lax.all_gather(features, 'row', axis=0, tiled=True)  243 us
    reduce_scatter x1, waiting for transfers between devices, per_device(): lax.psum_scatter(partial_value.astype(jnp.bfloat16), 'col', scatter_dimen...  181 us
    all_gather x1, waiting for transfers between devices, per_device(): grad_block = lax.all_gather(projected, 'col', axis=0, tiled=True)  123 us
  transfers between devices with their start and end apart: 4, of which 4 were waited for; matrix products, arithmetic and copies ran while one was open for 0% of the time, Pallas kernels for 0%

commit v1 on v0

v1 whole, which is shorter than its diff:
```python
import functools

import jax
import jax.numpy as jnp
from jax import lax
from jax.experimental import pallas as pl
from jax.experimental.pallas import tpu as pltpu
from jax.sharding import PartitionSpec as P

MESH = pl.DeviceIdType.MESH
F32 = jnp.float32
BF16 = jnp.bfloat16
NY, NX, NH, NP = 4, 4, 4, 8


def div(a, b):
    return lax.div(a, jnp.int32(b))


def rem(a, b):
    return lax.rem(a, jnp.int32(b))


class Spot:
    def __init__(self):
        self.row, self.col = lax.axis_index("row"), lax.axis_index("col")
        z = div(self.row, NY)
        odd = rem(z, 2)
        self.p = (1 - odd) * div(z, 2) + odd * div(15 - z, 2)
        self.y = rem(self.row, NY)
        self.h = div(self.col, NX * 2)
        self.x = rem(div(self.col, 2), NX)
        self.core = rem(self.col, 2)

    def row_of(self, dp, dy):
        p = rem(self.p + (dp + NP), NP)
        high = div(p, 4)
        z = (1 - high) * (2 * p) + high * (15 - 2 * p)
        return z * NY + rem(self.y + (dy + NY), NY)

    def row_device(self, dp, dy):
        return (self.row_of(dp, dy), self.col)

    def h_of(self, dh):
        return rem(self.h + (dh + NH), NH)

    def x_of(self, dx):
        return rem(self.x + (dx + NX), NX)

    def col_device(self, dh, dx, dcore):
        core = self.core if dcore == 0 else 1 - self.core
        return (self.row, (self.h_of(dh) * NX + self.x_of(dx)) * 2 + core)

    def row_neighbours(self):
        return [self.row_device(*d) for d in ((1, 0), (-1, 0), (0, 1), (0, -1))]

    def col_neighbours(self):
        steps = ((1, 0, 0), (-1, 0, 0), (0, 1, 0), (0, -1, 0), (0, 0, 1))
        return [self.col_device(*d) for d in steps]


def greet(neighbours):
    barrier = pltpu.get_barrier_semaphore()
    for device in neighbours:
        pl.semaphore_signal(barrier, inc=1, device_id=device, device_id_type=MESH)
    pl.semaphore_wait(barrier, len(neighbours))


class Wire:
    def __init__(self, send, recv):
        self.send, self.recv, self.started = send, recv, []

    def go(self, src, dst, device):
        n = len(self.started)
        copy = pltpu.make_async_remote_copy(
            src_ref=src,
            dst_ref=dst,
            send_sem=self.send.at[n],
            recv_sem=self.recv.at[n],
            device_id=device,
            device_id_type=MESH,
        )
        copy.start()
        self.started.append(copy)
        return copy

    def drain(self):
        for copy in self.started:
            copy.wait_send()


def halves(rows):
    return pl.ds(0, rows // 2), pl.ds(rows // 2, rows // 2)


GATHER_ROW_COPIES = 8 + 8 * 4


def gather_row(wire, at, own, block):
    top, low = halves(own.shape[0])
    right, left = at.row_device(1, 0), at.row_device(-1, 0)
    up, down = at.row_device(0, 1), at.row_device(0, -1)

    def spread(dp, src):
        place = block.at[at.row_of(dp, 0)]
        return dp, wire.go(src, place, up), wire.go(src, place, down)

    def pass_on(item):
        dp, from_below, from_above = item
        from_below.wait_recv()
        part = block.at[at.row_of(dp, -1), top]
        a = wire.go(part, part, up)
        from_above.wait_recv()
        part = block.at[at.row_of(dp, 1), low]
        return a, wire.go(part, part, down)

    mine = at.row_of(0, 0)
    fwd = wire.go(own, block.at[mine], right)
    bwd = wire.go(own, block.at[mine], left)
    spreading = [spread(0, own)]
    block[mine] = own[...]
    ends = []
    for s in (1, 2, 3):
        now = []
        fwd.wait_recv()
        t = at.row_of(-s, 0)
        part = block.at[t] if s < 3 else block.at[t, top]
        fwd = wire.go(part, part, right)
        now.append(spread(-s, block.at[t]))
        bwd.wait_recv()
        t = at.row_of(s, 0)
        part = block.at[t] if s < 3 else block.at[t, low]
        bwd = wire.go(part, part, left)
        now.append(spread(s, block.at[t]))
        ends += [pass_on(item) for item in spreading]
        spreading = now
    fwd.wait_recv()
    bwd.wait_recv()
    now = [spread(4, block.at[at.row_of(4, 0)])]
    ends += [pass_on(item) for item in spreading + now]
    for a, b in ends:
        a.wait_recv()
        b.wait_recv()


class Ring4:
    def __init__(self, wire, part, up, down, first_in, held, second_in):
        self.wire, self.part, self.up, self.down = wire, part, up, down
        self.first_in, self.held, self.second_in = first_in, held, second_in
        self.one, self.two = {}, {}
        self.top, self.low = halves(held.shape[2])

    def first(self, i):
        far = self.part(i, 2)
        self.one[i] = (
            self.wire.go(far.at[self.top], self.first_in.at[i, 0], self.up),
            self.wire.go(far.at[self.low], self.first_in.at[i, 1], self.down),
        )

    def second(self, i):
        top, low = self.top, self.low
        near = self.part(i, 1)
        self.held[i, 0, low] = near[low]
        self.one[i][0].wait_recv()
        self.held[i, 0, top] = add(near[top], self.first_in[i, 0])
        a = self.wire.go(self.held.at[i, 0], self.second_in.at[i, 0], self.up)
        near = self.part(i, -1)
        self.held[i, 1, top] = near[top]
        self.one[i][1].wait_recv()
        self.held[i, 1, low] = add(near[low], self.first_in[i, 1])
        self.two[i] = (a, self.wire.go(self.held.at[i, 1], self.second_in.at[i, 1], self.down))

    def third(self, i):
        for copy in self.two[i]:
            copy.wait_recv()
        return add3(self.part(i, 0)[...], self.second_in[i, 0], self.second_in[i, 1])


def add(a, b):
    return (a.astype(F32) + b.astype(F32)).astype(BF16)


def add3(a, b, c):
    return a.astype(F32) + b.astype(F32) + c.astype(F32)


SUM_ROW_COPIES = 8 * 4 + 8


def sum_row(wire, at, partial, out, first_in, held, second_in, half_in, half_out, full_in, full_out):
    order = (4, 3, -3, 2, -2, 1, -1, 0)
    rows = out.shape[0]
    mid = rows // 2
    right, left = at.row_device(1, 0), at.row_device(-1, 0)
    ring = Ring4(
        wire,
        lambda i, dy: partial.at[at.row_of(order[i], dy)],
        at.row_device(0, 1),
        at.row_device(0, -1),
        first_in,
        held,
        second_in,
    )
    last = {}

    def along_z(i, value):
        dp = order[i]
        if dp == 4:
            half_out[...] = value.astype(BF16)
            last[1] = wire.go(half_out.at[pl.ds(0, mid)], half_in.at[0], right)
            last[-1] = wire.go(half_out.at[pl.ds(mid, mid)], half_in.at[1], left)
        elif dp == 0:
            last[1].wait_recv()
            last[-1].wait_recv()
            out[...] = add3(value, full_in[2, 0], full_in[2, 1]).astype(BF16)
        else:
            way, step = (1, 0) if dp > 0 else (-1, 1)
            s = 3 - abs(dp)
            last[way].wait_recv()
            if s == 0:
                lo, hi = (0, mid) if way > 0 else (mid, rows)
                keep = (mid, rows) if way > 0 else (0, mid)
                full_out[s, step, lo:hi] = (value[lo:hi] + half_in[step].astype(F32)).astype(BF16)
                full_out[s, step, keep[0] : keep[1]] = value[keep[0] : keep[1]].astype(BF16)
            else:
                full_out[s, step] = (value + full_in[s - 1, step].astype(F32)).astype(BF16)
            last[way] = wire.go(full_out.at[s, step], full_in.at[s, step], right if way > 0 else left)

    ring.first(0)
    for t in range(len(order) + 1):
        if t + 1 < len(order):
            ring.first(t + 1)
        if t < len(order):
            ring.second(t)
        if t >= 1:
            along_z(t - 1, ring.third(t - 1))


def sum_row_scratch(rows, width):
    return [
        pltpu.VMEM((8, 2, rows // 2, width), BF16),
        pltpu.VMEM((8, 2, rows, width), BF16),
        pltpu.VMEM((8, 2, rows, width), BF16),
        pltpu.VMEM((2, rows // 2, width), BF16),
        pltpu.VMEM((rows, width), BF16),
        pltpu.VMEM((3, 2, rows, width), BF16),
        pltpu.VMEM((3, 2, rows, width), BF16),
    ]


SUM_COL_COPIES = 4 + 4 * 4 + 4


def sum_col(wire, at, partial, pair_in, paired, first_in, held, second_in, half_in, half_out, full_in, full_out):
    order = (2, 1, -1, 0)
    rows = partial.shape[3]
    mid = rows // 2
    right, left = at.col_device(1, 0, 0), at.col_device(-1, 0, 0)
    other = at.col_device(0, 0, 1)
    arriving = [
        wire.go(partial.at[at.h_of(dh), :, 1 - at.core], pair_in.at[i], other)
        for i, dh in enumerate(order)
    ]
    ring = Ring4(
        wire,
        lambda i, dx: paired.at[i, at.x_of(dx)],
        at.col_device(0, 1, 0),
        at.col_device(0, -1, 0),
        first_in,
        held,
        second_in,
    )

    def pair(i):
        arriving[i].wait_recv()
        paired[i] = add(partial[at.h_of(order[i]), :, at.core], pair_in[i])

    pair(0)
    ring.first(0)
    total, last = None, {}
    for t in range(5):
        if t + 1 < 4:
            pair(t + 1)
            ring.first(t + 1)
        if t < 4:
            ring.second(t)
        if t == 0:
            continue
        value = ring.third(t - 1)
        if t == 1:
            half_out[...] = value.astype(BF16)
            last[1] = wire.go(half_out.at[pl.ds(0, mid)], half_in.at[0], right)
            last[-1] = wire.go(half_out.at[pl.ds(mid, mid)], half_in.at[1], left)
        elif t < 4:
            full_out[t - 2] = value
        else:
            total = value
    last[1].wait_recv()
    full_in_f = wire_full(wire, full_out, half_in, full_in, 0, 0, mid, rows, right)
    last[-1].wait_recv()
    full_in_b = wire_full(wire, full_out, half_in, full_in, 1, mid, mid, rows, left)
    full_in_f.wait_recv()
    full_in_b.wait_recv()
    return add3(total, full_in[0], full_in[1])


def wire_full(wire, full_out, half_in, full_in, step, start, mid, rows, device):
    lo, keep = (slice(0, mid), slice(mid, rows)) if step == 0 else (slice(mid, rows), slice(0, mid))
    sent = full_in.at[2 + step]
    full_in[2 + step, lo] = (full_out[step, lo] + half_in[step].astype(F32)).astype(BF16)
    full_in[2 + step, keep] = full_out[step, keep].astype(BF16)
    return wire.go(sent, full_in.at[step], device)


def sum_col_scratch(rows, width):
    return [
        pltpu.VMEM((4, 4, rows, width), BF16),
        pltpu.VMEM((4, 4, rows, width), BF16),
        pltpu.VMEM((4, 2, rows // 2, width), BF16),
        pltpu.VMEM((4, 2, rows, width), BF16),
        pltpu.VMEM((4, 2, rows, width), BF16),
        pltpu.VMEM((2, rows // 2, width), BF16),
        pltpu.VMEM((rows, width), BF16),
        pltpu.VMEM((4, rows, width), BF16),
        pltpu.VMEM((2, rows, width), F32),
    ]


GATHER_COL_COPIES = 4 + 2 + 3 * 4 + 2 * 2 + 2 + 4


def gather_col(wire, at, own, block):
    rows = own.shape[0]
    top, low = halves(rows)
    right, left = at.col_device(1, 0, 0), at.col_device(-1, 0, 0)
    up, down = at.col_device(0, 1, 0), at.col_device(0, -1, 0)
    other = at.col_device(0, 0, 1)

    def place(dh, dx, part=None):
        ref = block.at[at.h_of(dh), at.x_of(dx), at.core]
        return ref if part is None else ref.at[part]

    block[at.h, at.x, at.core] = own[...]
    fwd_top = wire.go(own.at[top], place(0, 0, top), right)
    bwd_low = wire.go(own.at[low], place(0, 0, low), left)
    fwd_low = wire.go(own.at[low], place(0, 0, low), right)
    bwd_top = wire.go(own.at[top], place(0, 0, top), left)

    def spread(dh, src, part=None):
        return wire.go(src, place(dh, 0, part), up), wire.go(src, place(dh, 0, part), down)

    def pass_on(dh, item):
        item[0].wait_recv()
        part = place(dh, -1, top)
        a = wire.go(part, part, up)
        item[1].wait_recv()
        part = place(dh, 1, low)
        return a, wire.go(part, part, down)

    def across(dh, copies):
        for copy in copies:
            copy.wait_recv()
        part = block.at[at.h_of(dh), :, at.core]
        return wire.go(part, part, other)

    here = spread(0, own)
    here = pass_on(0, here)
    fwd_top.wait_recv()
    far_top = wire.go(place(-1, 0, top), place(-1, 0, top), right)
    bwd_low.wait_recv()
    far_low = wire.go(place(1, 0, low), place(1, 0, low), left)
    across_copies = [across(0, here)]
    fwd_low.wait_recv()
    behind = spread(-1, place(-1, 0))
    bwd_top.wait_recv()
    ahead = spread(1, place(1, 0))
    behind = pass_on(-1, behind)
    ahead = pass_on(1, ahead)
    across_copies.append(across(-1, behind))
    across_copies.append(across(1, ahead))
    far_top.wait_recv()
    tops = spread(2, place(2, 0, top), top)
    far_low.wait_recv()
    lows = spread(2, place(2, 0, low), low)
    tops[0].wait_recv()
    part = place(2, -1, top)
    a = wire.go(part, part, up)
    lows[1].wait_recv()
    part = place(2, 1, low)
    b = wire.go(part, part, down)
    across_copies.append(across(2, (tops[1], lows[0], a, b)))
    for copy in across_copies:
        copy.wait_recv()


def k_gather_row(own, block, send, recv):
    at = Spot()
    greet(at.row_neighbours())
    wire = Wire(send, recv)
    gather_row(wire, at, own, block)
    wire.drain()


def k_sum_row(partial, out, *scratch):
    *buffers, send, recv = scratch
    at = Spot()
    greet(at.row_neighbours())
    wire = Wire(send, recv)
    sum_row(wire, at, partial, out, *buffers)
    wire.drain()


def dense(aggregated, weight, out_grad, layer_out):
    v = jnp.dot(aggregated, weight[...], preferred_element_type=F32)
    c, d = 0.7978845608, 0.044715
    th = jnp.tanh(c * (v + d * v * v * v))
    layer_out[...] = (0.5 * v * (1.0 + th)).astype(BF16)
    slope = 0.5 * (1.0 + th) + 0.5 * v * (1.0 - th * th) * (c * (1.0 + (3.0 * d) * v * v))
    pre_grad = (out_grad[...].astype(F32) * slope).astype(BF16)
    return lax.dot_general(
        pre_grad, weight[...], (((1,), (1,)), ((), ())), preferred_element_type=F32
    ).astype(BF16)


def k_middle(partial, weight, out_grad, layer_out, block, projected, *scratch):
    *buffers, send, recv = scratch
    at = Spot()
    greet(at.col_neighbours())
    wire = Wire(send, recv)
    aggregated = sum_col(wire, at, partial, *buffers).astype(BF16)
    projected[...] = dense(aggregated, weight, out_grad, layer_out)
    gather_col(wire, at, projected, block)
    wire.drain()


VMEM_SPEC = pl.BlockSpec(memory_space=pltpu.VMEM)
LIMIT = 48 * 1024 * 1024


def remote(collective_id):
    return pltpu.CompilerParams(
        collective_id=collective_id, has_side_effects=True, vmem_limit_bytes=LIMIT
    )


def sems(n):
    return [pltpu.SemaphoreType.DMA((n,)), pltpu.SemaphoreType.DMA((n,))]


def call_gather_row(own):
    rows, width = own.shape
    return pl.pallas_call(
        k_gather_row,
        out_shape=jax.ShapeDtypeStruct((NP * NY, rows, width), BF16),
        in_specs=[VMEM_SPEC],
        out_specs=VMEM_SPEC,
        scratch_shapes=sems(GATHER_ROW_COPIES),
        compiler_params=remote(0),
        name="gather_row",
    )(own)


def call_sum_row(partial):
    _, rows, width = partial.shape
    return pl.pallas_call(
        k_sum_row,
        out_shape=jax.ShapeDtypeStruct((rows, width), BF16),
        in_specs=[VMEM_SPEC],
        out_specs=VMEM_SPEC,
        scratch_shapes=sum_row_scratch(rows, width) + sems(SUM_ROW_COPIES),
        compiler_params=remote(1),
        name="sum_row",
    )(partial)


def call_middle(partial, weight, out_grad):
    _, rows, width = partial.shape
    layer_out, block = pl.pallas_call(
        k_middle,
        out_shape=(
            jax.ShapeDtypeStruct((rows, width), BF16),
            jax.ShapeDtypeStruct((NH, NX, 2, rows, width), BF16),
        ),
        in_specs=[VMEM_SPEC] * 3,
        out_specs=(VMEM_SPEC, VMEM_SPEC),
        scratch_shapes=[pltpu.VMEM((rows, width), BF16)]
        + sum_col_scratch(rows, width)
        + sems(SUM_COL_COPIES + GATHER_COL_COPIES),
        compiler_params=remote(2),
        name="middle",
    )(partial.reshape(NH, NX, 2, rows, width), weight, out_grad)
    return layer_out, block.reshape(NH * NX * 2, rows, width)


def k_tiles(contract, to, source_at, count, tiles, source, out, total):
    total[...] = jnp.zeros_like(total)

    def slot(k, carry):
        product = lax.dot_general(
            tiles[k],
            source[source_at[k]],
            (((contract,), (0,)), ((), ())),
            preferred_element_type=F32,
        )
        total[to[k]] += product
        return carry

    lax.fori_loop(0, count[0], slot, 0)
    out[...] = total[...].astype(BF16)


def call_tiles(contract, to, source_at, count, tiles, source):
    smem = pl.BlockSpec(memory_space=pltpu.SMEM)
    return pl.pallas_call(
        functools.partial(k_tiles, contract),
        out_shape=jax.ShapeDtypeStruct(source.shape, BF16),
        in_specs=[smem] * 3 + [VMEM_SPEC] * 2,
        out_specs=VMEM_SPEC,
        scratch_shapes=[pltpu.VMEM(source.shape, F32)],
        compiler_params=pltpu.CompilerParams(vmem_limit_bytes=LIMIT),
        name="tiles" + str(contract),
    )(to, source_at, count, tiles, source)


def per_device(features, tile_values, tile_rows, tile_cols, tile_count, weight, out_grad):
    tiles = tile_values[0, 0]
    row_index, col_index, count = tile_rows[0, 0], tile_cols[0, 0], tile_count[0]
    source = call_gather_row(features)
    partial = call_tiles(1, row_index, col_index, count, tiles, source)
    layer_out, grads = call_middle(partial, weight, out_grad)
    back = call_tiles(0, col_index, row_index, count, tiles, grads)
    return layer_out, call_sum_row(back)


def solution(mesh):
    in_specs = (
        P(("col", "row"), None),
        P("row", "col", None, None, None),
        P("row", "col", None),
        P("row", "col", None),
        P("row", "col"),
        P(),
        P(("row", "col"), None),
    )
    out_specs = (P(("row", "col"), None), P(("col", "row"), None))
    return jax.shard_map(
        per_device, mesh=mesh, in_specs=in_specs, out_specs=out_specs, check_vma=False
    )
```

time: 850 us -> 166 us (0.20)
  waiting for transfers between devices: 790 us -> 0 us
  Pallas kernels: 0 us -> 162 us
  other arithmetic: 25.4 us -> 0 us
  between operations: 14.4 us -> 1.46 us
  local copies, waits for them, and re-layouts: 11.7 us -> 2.12 us
    reduce_scatter x2 -> x0, waiting for transfers between devices: 424 us -> none  [the longest x1 243 us: per_device(): lax.psum_scatter(back_partial.astype(jnp.bfloat16), 'row', scatter_dimens...]
    all_gather x2 -> x0, waiting for transfers between devices: 366 us -> none  [the longest x1 243 us: per_device(): source_block = lax.all_gather(features, 'row', axis=0, tiled=True)]
    pallas_call x0 -> x5, Pallas kernels: none -> 162 us  [the longest x1 90.2 us: call_middle(): pl.pallas_call(k_middle, out_shape=(jax.ShapeDtypeStruct((rows, width), B...]
    scatter-add x2 -> x0, other arithmetic: 16.4 us -> none  [place_tiles(): jnp.zeros((count_tiles, tile_len, width), jnp.float32).at[indices]]
  transfers between devices with their start and end apart: 4 -> 0, of which waited for: 4 -> 0; matrix products, arithmetic and copies ran while one was open for 0% -> 0% of each run, Pallas kernels for 0% -> 0%
where the time goes in v1:
time: 166 us; the launch traced here: 165 us
  Pallas kernels  162 us (98%)
  local copies, waits for them, and re-layouts  2.12 us (1%)
    pallas_call x1, Pallas kernels, call_middle(): pl.pallas_call(k_middle, out_shape=(jax.ShapeDtypeStruct((rows, width), B...  90.2 us
    pallas_call x1, Pallas kernels, call_gather_row(): pl.pallas_call(k_gather_row, out_shape=jax.ShapeDtypeStruct((NP * NY, row...  36.2 us
    pallas_call x1, Pallas kernels, call_sum_row(): pl.pallas_call(k_sum_row, out_shape=jax.ShapeDtypeStruct((rows, width), B...  30.4 us
    pallas_call x2, Pallas kernels, call_tiles(): pl.pallas_call(functools.partial(k_tiles, contract), out_shape=jax.ShapeD...  4.84 us

profile of v1, /device:TPU:6, one launch (start us, length us, event | category | flops | bytes accessed | tf_op | source)
XLA Modules:
  0.0 165.2 jit_solution(15327765707400239183)
XLA Ops:
  0.6 0.0 copy-start
  1.4 0.0 copy-start.2
  1.4 0.8 copy-done.2
  2.2 0.0 copy-start.4
  2.2 0.0 copy-start.5
  2.2 36.2 %gather_row.1.source = bf16[32,128,256]{2,1,0:T(8,128)(2,1)S(1)} custom-call(bf16[128,256]{1,0:T(8,128)(2,1)S(1)} %copy-done.2), custom_call_target="tpu_custom_call" | custom-call | tf_op jit(solution)/shard_map/gather_row/pallas_call | solution.py:452
  38.4 0.0 copy-done
  38.4 0.0 copy-done.4
  38.4 0.0 copy-done.5
  38.5 0.0 copy-start.1
  38.5 0.0 copy-start.3
  38.5 2.2 %tiles1.1 = bf16[32,128,256]{2,1,0:T(8,128)(2,1)S(1)} custom-call(s32[24]{0:T(128)S(1)} %bitcast.12, s32[24]{0:T(128)S(1)} %bitcast.14, s32[1]{0:T(128)} %bitcast.6.count, bf16[24,128,128]{2,1,0:T(8,128)(2,1)S(1)} %bitcast.9, bf16[32,128,256]{2,1,0:T(8,128)(2,1)S(1)} %gather_row.1.source), custom_call_target="tpu_custom_call" | custom-call | tf_op jit(solution)/shard_map/tiles1/pallas_call | solution.py:514
  40.7 0.0 copy-done.1
  40.7 0.0 copy-done.3
  40.7 90.2 %middle.1 = (bf16[128,256]{1,0:T(8,128)(2,1)S(1)}, bf16[4,4,2,128,256]{4,3,2,1,0:T(8,128)(2,1)S(1)}) custom-call(bf16[4,4,2,128,256]{4,3,2,1,0:T(8,128)(2,1)S(1)} %bitcast.8, bf16[256,256]{1,0:T(8,128)(2,1)S(1)} %copy-done.1, bf16[128,256]{1,0:T(8,128)(2,1)S(1)} %copy-done.3), custom_call_target="tpu_custom_call" | custom-call | tf_op jit(solution)/shard_map/middle/pallas_call | solution.py:478
  130.9 2.6 %tiles0.1.partial = bf16[32,128,256]{2,1,0:T(8,128)(2,1)S(1)} custom-call(s32[24]{0:T(128)S(1)} %bitcast.15, s32[24]{0:T(128)S(1)} %bitcast.13, s32[1]{0:T(128)} %bitcast.7.count, bf16[24,128,128]{2,1,0:T(8,128)(2,1)S(1)} %bitcast.10, bf16[32,128,256]{2,1,0:T(8,128)(2,1)S(1)} %bitcast.11), custom_call_target="tpu_custom_call" | custom-call | tf_op jit(solution)/shard_map/tiles0/pallas_call | solution.py:514
  133.5 30.4 %sum_row.1 = bf16[128,256]{1,0:T(8,128)(2,1)S(1)} custom-call(bf16[32,128,256]{2,1,0:T(8,128)(2,1)S(1)} %tiles0.1.partial), custom_call_target="tpu_custom_call" | custom-call | tf_op jit(solution)/shard_map/sum_row/pallas_call | solution.py:465
  163.9 0.6 copy.12
  164.6 0.6 copy.13
Async XLA Ops:
  0.6 37.8 %copy-start = (bf16[1,1,24,128,128]{4,3,2,1,0:T(8,128)(2,1)S(1)}, bf16[1,1,24,128,128]{4,3,2,1,0:T(8,128)(2,1)}, u32[]{:S(2)}) copy-start(bf16[1,1,24,128,128]{4,3,2,1,0:T(8,128)(2,1)} %param.8) | copy-start | bytes 2359300
  1.4 0.8 copy-start.2
  2.2 36.2 %copy-start.4 = (s32[1,1,24]{2,1,0:T(1,128)S(1)}, s32[1,1,24]{2,1,0:T(1,128)}, u32[]{:S(2)}) copy-start(s32[1,1,24]{2,1,0:T(1,128)} %param.9) | copy-start | bytes 292
  2.2 36.2 %copy-start.5 = (s32[1,1,24]{2,1,0:T(1,128)S(1)}, s32[1,1,24]{2,1,0:T(1,128)}, u32[]{:S(2)}) copy-start(s32[1,1,24]{2,1,0:T(1,128)} %param.10) | copy-start | bytes 292
  38.5 2.3 %copy-start.1 = (bf16[256,256]{1,0:T(8,128)(2,1)S(1)}, bf16[256,256]{1,0:T(8,128)(2,1)}, u32[]{:S(2)}) copy-start(bf16[256,256]{1,0:T(8,128)(2,1)} %weight.1) | copy-start | bytes 393220
  38.5 2.3 %copy-start.3 = (bf16[128,256]{1,0:T(8,128)(2,1)S(1)}, bf16[128,256]{1,0:T(8,128)(2,1)}, u32[]{:S(2)}) copy-start(bf16[128,256]{1,0:T(8,128)(2,1)} %out_grad.1) | copy-start | bytes 196612

commit v2 on v0

v2 whole, which is shorter than its diff:
```python
import jax
import jax.numpy as jnp
from jax import lax
from jax.experimental import pallas as pl
from jax.experimental.pallas import tpu as pltpu
from jax.sharding import PartitionSpec as P

MESH = pl.DeviceIdType.MESH
F32 = jnp.float32
BF16 = jnp.bfloat16
NY, NX, NH, NP = 4, 4, 4, 8
ROWS = NP * NY
COLS = NH * NX * 2


def div(a, b):
    return lax.div(a, jnp.int32(b))


def rem(a, b):
    return lax.rem(a, jnp.int32(b))


class Spot:
    def __init__(self):
        self.row, self.col = lax.axis_index("row"), lax.axis_index("col")
        z = div(self.row, NY)
        odd = rem(z, 2)
        self.p = (1 - odd) * div(z, 2) + odd * div(15 - z, 2)
        self.y = rem(self.row, NY)
        self.h = div(self.col, NX * 2)
        self.x = rem(div(self.col, 2), NX)
        self.core = rem(self.col, 2)

    def row_of(self, dp, dy):
        p = rem(self.p + (dp + NP), NP)
        high = div(p, 4)
        z = (1 - high) * (2 * p) + high * (15 - 2 * p)
        return z * NY + rem(self.y + (dy + NY), NY)

    def row_device(self, dp, dy):
        return (self.row_of(dp, dy), self.col)

    def h_of(self, dh):
        return rem(self.h + (dh + NH), NH)

    def x_of(self, dx):
        return rem(self.x + (dx + NX), NX)

    def col_device(self, dh, dx, dcore):
        core = self.core if dcore == 0 else 1 - self.core
        return (self.row, (self.h_of(dh) * NX + self.x_of(dx)) * 2 + core)

    def slot(self, dh, dx, dcore=0):
        core = self.core if dcore == 0 else 1 - self.core
        return core * (NH * NX) + self.h_of(dh) * NX + self.x_of(dx)

    def row_neighbours(self):
        return [self.row_device(*d) for d in ((1, 0), (-1, 0), (0, 1), (0, -1), (0, 2))]

    def col_neighbours(self):
        steps = ((1, 0, 0), (-1, 0, 0), (0, 1, 0), (0, -1, 0), (0, 2, 0), (0, 0, 1))
        return [self.col_device(*d) for d in steps]


def greet(neighbours):
    barrier = pltpu.get_barrier_semaphore()
    for device in neighbours:
        pl.semaphore_signal(barrier, inc=1, device_id=device, device_id_type=MESH)
    pl.semaphore_wait(barrier, len(neighbours))


class Wire:
    def __init__(self, send, recv):
        self.send, self.recv, self.started = send, recv, []

    def go(self, src, dst, device):
        n = len(self.started)
        copy = pltpu.make_async_remote_copy(
            src_ref=src,
            dst_ref=dst,
            send_sem=self.send.at[n],
            recv_sem=self.recv.at[n],
            device_id=device,
            device_id_type=MESH,
        )
        copy.start()
        self.started.append(copy)
        return copy

    def drain(self):
        for copy in self.started:
            copy.wait_send()


def halves(rows):
    return pl.ds(0, rows // 2), pl.ds(rows // 2, rows // 2)


GATHER_ROW_COPIES = 14 + 5 * 6 + 3 * 6


def gather_row(wire, at, own, block):
    part = halves(own.shape[0])
    along = (at.row_device(1, 0), at.row_device(-1, 0))
    up, down, far = at.row_device(0, 1), at.row_device(0, -1), at.row_device(0, 2)

    def place(dp, dy, half):
        return block.at[at.row_of(dp, dy), part[half]]

    ends = []

    def spread(dp, half, src, direct):
        dst = place(dp, 0, half)
        a, b = wire.go(src, dst, up), wire.go(src, dst, down)
        if direct:
            ends.extend((a, b, wire.go(src, dst, far)))
            return None
        return dp, half, a, b

    def pass_on(item):
        dp, half, a, b = item
        if half == 0:
            a.wait_recv()
            ref = place(dp, -1, 0)
            ends.extend((b, wire.go(ref, ref, up)))
        else:
            b.wait_recv()
            ref = place(dp, 1, 1)
            ends.extend((a, wire.go(ref, ref, down)))

    moving = {}
    for half in (0, 1):
        for way in (0, 1):
            now = half if way == 0 else 1 - half
            moving[way, now] = wire.go(own.at[part[now]], place(0, 0, now), along[way])
    spreading = [spread(0, half, own.at[part[half]], False) for half in (0, 1)]
    block[at.row_of(0, 0)] = own[...]
    for s in (1, 2, 3, 4):
        now = []
        for half in (0, 1):
            for way in (0, 1):
                part_now = half if way == 0 else 1 - half
                copy = moving.pop((way, part_now), None)
                if copy is None:
                    continue
                copy.wait_recv()
                dp = -s if way == 0 else s
                ref = place(dp, 0, part_now)
                if s < 3 or (s == 3 and part_now == way):
                    moving[way, part_now] = wire.go(ref, ref, along[way])
                now.append(spread(dp, part_now, ref, s >= 3))
        for item in spreading:
            if item is not None:
                pass_on(item)
        spreading = now
    for copy in ends:
        copy.wait_recv()


def add(a, b):
    return (a.astype(F32) + b.astype(F32)).astype(BF16)


SUM_ROW_COPIES = 3 * 3 + 5 * 6 + 14
DIRECT = 3


def sum_row(wire, at, block_of, out, mine, direct_in, first_in, held, second_in, total, z_in, z_out):
    order = (4, 3, -3, 2, -2, 1, -1, 0)
    rows = out.shape[0]
    cut = (slice(0, rows // 2), slice(rows // 2, rows))
    part = halves(rows)
    along = (at.row_device(1, 0), at.row_device(-1, 0))
    up, down, far = at.row_device(0, 1), at.row_device(0, -1), at.row_device(0, 2)
    flight = {}

    def first(i):
        for dy in (2, 1, -1):
            mine[i, dy % NY] = block_of(at.row_of(order[i], dy)).astype(BF16)
        if i < DIRECT:
            flight[i] = (
                wire.go(mine.at[i, 2], direct_in.at[i, 2], far),
                wire.go(mine.at[i, 1], direct_in.at[i, 0], up),
                wire.go(mine.at[i, 3], direct_in.at[i, 1], down),
            )
            return
        k = i - DIRECT
        flight[i] = [
            wire.go(mine.at[i, 2, part[0]], first_in.at[k, 0], up),
            wire.go(mine.at[i, 2, part[1]], first_in.at[k, 1], down),
            wire.go(mine.at[i, 1, part[1]], second_in.at[k, 0, part[1]], up),
            wire.go(mine.at[i, 3, part[0]], second_in.at[k, 1, part[0]], down),
        ]

    def second(i):
        k = i - DIRECT
        flight[i][0].wait_recv()
        held[k, 0] = add(mine[i, 1, cut[0]], first_in[k, 0])
        flight[i].append(wire.go(held.at[k, 0], second_in.at[k, 0, part[0]], up))
        flight[i][1].wait_recv()
        held[k, 1] = add(mine[i, 3, cut[1]], first_in[k, 1])
        flight[i].append(wire.go(held.at[k, 1], second_in.at[k, 1, part[1]], down))

    def third(i):
        value = block_of(at.row_of(order[i], 0))
        if i < DIRECT:
            for copy in flight[i]:
                copy.wait_recv()
            for n in range(3):
                value += direct_in[i, n].astype(F32)
        else:
            for copy in flight[i][2:]:
                copy.wait_recv()
            for n in range(2):
                value += second_in[i - DIRECT, n].astype(F32)
        total[i] = value

    moving = {}

    def send(way, half, step):
        moving[way, half] = wire.go(z_out.at[way, half, step], z_in.at[way, half, step], along[way])

    def start(i, way, half, step):
        z_out[way, half, step] = total[i, cut[half]].astype(BF16)
        send(way, half, step)

    def carry(i, way, half, step):
        moving[way, half].wait_recv()
        z_out[way, half, step] = (total[i, cut[half]] + z_in[way, half, step - 1].astype(F32)).astype(BF16)
        send(way, half, step)

    for i in range(4):
        first(i)
    third(0)
    start(0, 0, 0, 0)
    start(0, 1, 1, 0)
    first(4)
    third(1)
    start(1, 0, 1, 1)
    third(2)
    start(2, 1, 0, 1)
    first(5)
    second(3)
    carry(1, 0, 0, 1)
    carry(2, 1, 1, 1)
    first(6)
    second(4)
    first(7)
    third(3)
    third(4)
    for step, i in ((2, 3), (3, 5)):
        for half in (0, 1):
            carry(i, 0, 1 - half, step)
            carry(i + 1, 1, half, step)
        if step == 2:
            for n in (5, 6, 7):
                second(n)
            third(5)
            third(6)
    third(7)
    for half in (0, 1):
        value = total[7, cut[half]]
        for way in (0, 1):
            moving[way, half].wait_recv()
            value += z_in[way, half, 3].astype(F32)
        out[cut[half]] = value.astype(BF16)


def sum_row_scratch(rows, width):
    mid = rows // 2
    return [
        pltpu.VMEM((8, 4, rows, width), BF16),
        pltpu.VMEM((DIRECT, 3, rows, width), BF16),
        pltpu.VMEM((8 - DIRECT, 2, mid, width), BF16),
        pltpu.VMEM((8 - DIRECT, 2, mid, width), BF16),
        pltpu.VMEM((8 - DIRECT, 2, rows, width), BF16),
        pltpu.VMEM((8, rows, width), F32),
        pltpu.VMEM((2, 2, 4, mid, width), BF16),
        pltpu.VMEM((2, 2, 4, mid, width), BF16),
    ]


SUM_COL_COPIES = 4 + 4 * 3 + 6


def sum_col(wire, at, block_of, pair_out, pair_in, paired, x_in, total, z_in, z_out):
    order = (2, 1, -1, 0)
    rows = total.shape[1]
    mid = rows // 2
    cut = (slice(0, mid), slice(mid, rows))
    part = halves(rows)
    along = (at.col_device(1, 0, 0), at.col_device(-1, 0, 0))
    up, down, far = at.col_device(0, 1, 0), at.col_device(0, -1, 0), at.col_device(0, 2, 0)
    other = at.col_device(0, 0, 1)
    crossing, flight = [], []
    for i, dh in enumerate(order):
        for dx in range(NX):
            pair_out[i, dx] = block_of(at.slot(dh, dx, 1)).astype(BF16)
        crossing.append(wire.go(pair_out.at[i], pair_in.at[i], other))
    for i, dh in enumerate(order):
        crossing[i].wait_recv()
        copies = []
        for dx, n, device in ((2, 2, far), (1, 0, up), (3, 1, down)):
            paired[i, dx] = add(block_of(at.slot(dh, dx)), pair_in[i, dx])
            copies.append(wire.go(paired.at[i, dx], x_in.at[i, n], device))
        flight.append(copies)

    def third(i):
        value = block_of(at.slot(order[i], 0)) + pair_in[i, 0].astype(F32)
        for copy in flight[i]:
            copy.wait_recv()
        for n in range(3):
            value += x_in[i, n].astype(F32)
        total[i] = value

    moving = {}

    def send(way, half, step):
        moving[way, half] = wire.go(z_out.at[way, half, step], z_in.at[way, half, step], along[way])

    def start(i, way, half, step):
        z_out[way, half, step] = total[i, cut[half]].astype(BF16)
        send(way, half, step)

    def carry(i, way, half, step):
        moving[way, half].wait_recv()
        z_out[way, half, step] = (total[i, cut[half]] + z_in[way, half, step - 1].astype(F32)).astype(BF16)
        send(way, half, step)

    third(0)
    start(0, 0, 0, 0)
    start(0, 1, 1, 0)
    third(1)
    start(1, 0, 1, 1)
    third(2)
    start(2, 1, 0, 1)
    third(3)
    carry(1, 0, 0, 1)
    carry(2, 1, 1, 1)
    for half in (0, 1):
        value = total[3, cut[half]]
        for way in (0, 1):
            moving[way, half].wait_recv()
            value += z_in[way, half, 1].astype(F32)
        total[3, cut[half]] = value
    return total[3]


def sum_col_scratch(rows, width):
    mid = rows // 2
    return [
        pltpu.VMEM((4, 4, rows, width), BF16),
        pltpu.VMEM((4, 4, rows, width), BF16),
        pltpu.VMEM((4, 4, rows, width), BF16),
        pltpu.VMEM((4, 3, rows, width), BF16),
        pltpu.VMEM((4, rows, width), F32),
        pltpu.VMEM((2, 2, 2, mid, width), BF16),
        pltpu.VMEM((2, 2, 2, mid, width), BF16),
    ]


GATHER_COL_COPIES = 6 + 8 * 3 + 8


def gather_col(wire, at, own, block):
    part = halves(own.shape[0])
    along = (at.col_device(1, 0, 0), at.col_device(-1, 0, 0))
    near = (at.col_device(0, 2, 0), at.col_device(0, 1, 0), at.col_device(0, -1, 0))
    other = at.col_device(0, 0, 1)

    def place(dh, half):
        return block.at[at.slot(dh, 0), part[half]]

    moving = {}
    for way, half in ((0, 0), (1, 1), (0, 1), (1, 0)):
        moving[way, half] = wire.go(own.at[part[half]], place(0, half), along[way])
    block[at.slot(0, 0)] = own[...]

    def spread(dh, half):
        ref = place(dh, half)
        return dh, half, [wire.go(ref, ref, device) for device in near]

    crossed = []

    def across(item):
        dh, half, copies = item
        for copy in copies:
            copy.wait_recv()
        first = at.core * (NH * NX) + at.h_of(dh) * NX
        ref = block.at[pl.ds(first, NX), part[half]]
        crossed.append(wire.go(ref, ref, other))

    def arrive(way, half, dh):
        moving[way, half].wait_recv()
        if abs(dh) == 1 and half == way:
            ref = place(dh, half)
            moving[way, half] = wire.go(ref, ref, along[way])
        return spread(dh, half)

    here = [spread(0, half) for half in (0, 1)]
    for item in here:
        across(item)
    early = [arrive(0, 0, -1), arrive(1, 1, 1)]
    late = [arrive(0, 1, -1), arrive(1, 0, 1)]
    for item in early:
        across(item)
    last = [arrive(0, 0, 2)]
    for item in late:
        across(item)
    last.append(arrive(1, 1, 2))
    for item in last:
        across(item)
    for copy in crossed:
        copy.wait_recv()


def dense(aggregated, weight, out_grad, layer_out):
    v = jnp.dot(aggregated, weight[...], preferred_element_type=F32)
    c, d = 0.7978845608, 0.044715
    th = jnp.tanh(c * (v + d * v * v * v))
    layer_out[...] = (0.5 * v * (1.0 + th)).astype(BF16)
    slope = 0.5 * (1.0 + th) + 0.5 * v * (1.0 - th * th) * (c * (1.0 + (3.0 * d) * v * v))
    pre_grad = (out_grad[...].astype(F32) * slope).astype(BF16)
    return lax.dot_general(
        pre_grad, weight[...], (((1,), (1,)), ((), ())), preferred_element_type=F32
    ).astype(BF16)


def tile_sums(contract, tiles, source, source_at, before, sums):
    slots = tiles.shape[0]
    group = 4

    def some(g, carry):
        for n in range(group):
            k = g * group + n
            product = lax.dot_general(
                tiles[k],
                source[source_at[k]],
                (((contract,), (0,)), ((), ())),
                preferred_element_type=F32,
            )
            sums[k] = product + sums[before[k]]
        return carry

    lax.fori_loop(0, slots // group, some, 0)


def k_plan(rows, cols, count, row_slot, row_before, row_last, col_before, col_last):
    slots = rows.shape[0]

    def clear(t, carry):
        row_last[t] = jnp.int32(slots)
        col_last[t] = jnp.int32(slots)
        return carry

    lax.fori_loop(0, ROWS, clear, 0)

    def slot(k, carry):
        r, c = rows[k], cols[k]
        s = rem(r, 2) * (NH * NX) + div(r, 2)
        row_slot[k] = s
        live = k < count[0]
        old_row, old_col = row_last[s], col_last[c]
        row_before[k], col_before[k] = old_row, old_col
        row_last[s] = jnp.where(live, k, old_row)
        col_last[c] = jnp.where(live, k, old_col)
        return carry

    lax.fori_loop(0, slots, slot, 0)


SMEM_SPEC = pl.BlockSpec(memory_space=pltpu.SMEM)
VMEM_SPEC = pl.BlockSpec(memory_space=pltpu.VMEM)
ANY_SPEC = pl.BlockSpec(memory_space=pl.ANY)
LIMIT = 56 * 1024 * 1024


def plan(rows, cols, count):
    slots = rows.shape[0]
    one = jax.ShapeDtypeStruct((slots,), jnp.int32)
    table = jax.ShapeDtypeStruct((ROWS,), jnp.int32)
    return pl.pallas_call(
        k_plan,
        out_shape=(one, one, table, one, table),
        in_specs=[SMEM_SPEC] * 3,
        out_specs=(SMEM_SPEC,) * 5,
        name="plan",
    )(rows, cols, count)


def k_layer(
    col_at, row_slot, row_before, row_last, col_before, col_last,
    own, tiles_hbm, weight, out_grad, layer_out, grad_x, *scratch
):
    tiles, tile_sem, source, grads, projected, sums, *scratch = scratch
    n_row, n_col = len(sum_row_scratch(32, 128)), len(sum_col_scratch(32, 128))
    row_buffers, col_buffers = scratch[:n_row], scratch[n_row : n_row + n_col]
    send, recv = scratch[n_row + n_col :]
    at = Spot()
    load = pltpu.make_async_copy(tiles_hbm, tiles, tile_sem)
    load.start()
    sums[tiles.shape[0]] = jnp.zeros(sums.shape[1:], F32)
    greet(at.row_neighbours() + at.col_neighbours())
    wire = Wire(send, recv)
    gather_row(wire, at, own, source)
    load.wait()
    tile_sums(1, tiles, source, col_at, row_before, sums)
    aggregated = sum_col(wire, at, lambda slot: sums[row_last[slot]], *col_buffers)
    projected[...] = dense(aggregated.astype(BF16), weight, out_grad, layer_out)
    gather_col(wire, at, projected, grads)
    tile_sums(0, tiles, grads, row_slot, col_before, sums)
    sum_row(wire, at, lambda row: sums[col_last[row]], grad_x, *row_buffers)
    wire.drain()


def layer(tables, own, tiles, weight, out_grad):
    rows, width = own.shape
    slots = tiles.shape[0]
    block = jax.ShapeDtypeStruct((rows, width), BF16)
    copies = GATHER_ROW_COPIES + SUM_COL_COPIES + GATHER_COL_COPIES + SUM_ROW_COPIES
    return pl.pallas_call(
        k_layer,
        out_shape=(block, block),
        in_specs=[SMEM_SPEC] * 6 + [VMEM_SPEC, ANY_SPEC, VMEM_SPEC, VMEM_SPEC],
        out_specs=(VMEM_SPEC, VMEM_SPEC),
        scratch_shapes=[
            pltpu.VMEM(tiles.shape, BF16),
            pltpu.SemaphoreType.DMA,
            pltpu.VMEM((ROWS, rows, width), BF16),
            pltpu.VMEM((COLS, rows, width), BF16),
            pltpu.VMEM((rows, width), BF16),
            pltpu.VMEM((slots + 1, rows, width), F32),
        ]
        + sum_row_scratch(rows, width)
        + sum_col_scratch(rows, width)
        + [pltpu.SemaphoreType.DMA((copies,)), pltpu.SemaphoreType.DMA((copies,))],
        compiler_params=pltpu.CompilerParams(
            collective_id=0, has_side_effects=True, vmem_limit_bytes=LIMIT
        ),
        name="layer",
    )(*tables, own, tiles, weight, out_grad)


def per_device(features, tile_values, tile_rows, tile_cols, tile_count, weight, out_grad):
    rows, cols = tile_rows[0, 0], tile_cols[0, 0]
    tables = plan(rows, cols, tile_count[0])
    return layer((cols,) + tuple(tables), features, tile_values[0, 0], weight, out_grad)


def solution(mesh):
    in_specs = (
        P(("col", "row"), None),
        P("row", "col", None, None, None),
        P("row", "col", None),
        P("row", "col", None),
        P("row", "col"),
        P(),
        P(("row", "col"), None),
    )
    out_specs = (P(("row", "col"), None), P(("col", "row"), None))
    return jax.shard_map(
        per_device, mesh=mesh, in_specs=in_specs, out_specs=out_specs, check_vma=False
    )
```

time: 850 us -> 152 us (0.18)
  the two profiles are of different devices: /device:TPU:6 before, /device:TPU:1 now
where the time goes in v2:
time: 152 us
  Pallas kernels  148 us (97%)
  local copies, waits for them, and re-layouts  2.14 us (1%)
    pallas_call x1, Pallas kernels, layer(): pl.pallas_call(k_layer, out_shape=(block, block), in_specs=[SMEM_SPEC] *...  146 us

profile of v2, /device:TPU:1, one launch (start us, length us, event | category | flops | bytes accessed | tf_op | source)
XLA Modules:
  0.0 151.7 jit_solution(5659948344063914591)
XLA Ops:
  1.3 1.9 %plan.1 = (s32[24]{0:T(128)}, s32[24]{0:T(128)}, s32[32]{0:T(128)}, s32[24]{0:T(128)}, s32[32]{0:T(128)}) custom-call(s32[24]{0:T(128)} %bitcast.8, s32[24]{0:T(128)} %bitcast.6, s32[1]{0:T(128)} %bitcast.4.count), custom_call_target="tpu_custom_call" | custom-call | tf_op jit(solution)/shard_map/plan/pallas_call | solution.py:483
  3.2 146.4 %layer.1 = (bf16[128,256]{1,0:T(8,128)(2,1)}, bf16[128,256]{1,0:T(8,128)(2,1)}) custom-call(s32[24]{0:T(128)} %bitcast.7, s32[24]{0:T(128)} %get-tuple-element.7.row_slot, s32[24]{0:T(128)} %get-tuple-element.8.row_before, s32[32]{0:T(128)} %get-tuple-element.9.row_last, s32[24]{0:T(128)} %get-tuple-element.10.col_before, s32[32]{0:T(128)} %get-tuple-element.11.col_last, ...), custom_call_target="tpu_custom_call" | custom-call | tf_op jit(solution)/shard_map/layer/pallas_call | solution.py:522
  149.6 0.0 copy-start
  149.6 1.5 copy.12
  151.1 0.0 copy-done
  151.1 0.6 copy.13
Async XLA Ops:
  149.6 1.5 %copy-start = (bf16[128,256]{1,0:T(8,128)(2,1)S(1)}, bf16[128,256]{1,0:T(8,128)(2,1)}, u32[]{:S(2)}) copy-start(bf16[128,256]{1,0:T(8,128)(2,1)} %get-tuple-element.15) | copy-start | bytes 196612

commit v3 on v2

--- a/solution.py
+++ b/solution.py
@@ -68,6 +68,17 @@
     for device in neighbours:
         pl.semaphore_signal(barrier, inc=1, device_id=device, device_id_type=MESH)
     pl.semaphore_wait(barrier, len(neighbours))
+
+
+class Copy:
+    def __init__(self, copy):
+        self.copy, self.gone = copy, False
+        self.wait_recv = copy.wait_recv
+
+    def left(self):
+        if not self.gone:
+            self.copy.wait_send()
+            self.gone = True
 
 
 class Wire:
@@ -85,12 +96,12 @@
             device_id_type=MESH,
         )
         copy.start()
-        self.started.append(copy)
-        return copy
+        self.started.append(Copy(copy))
+        return self.started[-1]
 
     def drain(self):
         for copy in self.started:
-            copy.wait_send()
+            copy.left()
 
 
 def halves(rows):
@@ -178,6 +189,9 @@
     def first(i):
         for dy in (2, 1, -1):
             mine[i, dy % NY] = block_of(at.row_of(order[i], dy)).astype(BF16)
+        if i > 0:
+            for copy in flight[max(0, i - 2)]:
+                copy.left()
         if i < DIRECT:
             flight[i] = (
                 wire.go(mine.at[i, 2], direct_in.at[i, 2], far),
@@ -230,25 +244,28 @@
         z_out[way, half, step] = (total[i, cut[half]] + z_in[way, half, step - 1].astype(F32)).astype(BF16)
         send(way, half, step)
 
-    for i in range(4):
+    for i in range(3):
         first(i)
     third(0)
     start(0, 0, 0, 0)
     start(0, 1, 1, 0)
+    first(3)
+    third(1)
+    moving[0, 0].left()
+    start(1, 0, 1, 1)
     first(4)
-    third(1)
-    start(1, 0, 1, 1)
     third(2)
+    moving[1, 1].left()
     start(2, 1, 0, 1)
-    first(5)
     second(3)
     carry(1, 0, 0, 1)
     carry(2, 1, 1, 1)
+    first(5)
+    second(4)
     first(6)
-    second(4)
-    first(7)
     third(3)
     third(4)
+    first(7)
     for step, i in ((2, 3), (3, 5)):
         for half in (0, 1):
             carry(i, 0, 1 - half, step)
@@ -294,17 +311,25 @@
     up, down, far = at.col_device(0, 1, 0), at.col_device(0, -1, 0), at.col_device(0, 2, 0)
     other = at.col_device(0, 0, 1)
     crossing, flight = [], []
-    for i, dh in enumerate(order):
+
+    def cross(i):
         for dx in range(NX):
-            pair_out[i, dx] = block_of(at.slot(dh, dx, 1)).astype(BF16)
+            pair_out[i, dx] = block_of(at.slot(order[i], dx, 1)).astype(BF16)
         crossing.append(wire.go(pair_out.at[i], pair_in.at[i], other))
-    for i, dh in enumerate(order):
+
+    def first(i):
         crossing[i].wait_recv()
-        copies = []
-        for dx, n, device in ((2, 2, far), (1, 0, up), (3, 1, down)):
-            paired[i, dx] = add(block_of(at.slot(dh, dx)), pair_in[i, dx])
-            copies.append(wire.go(paired.at[i, dx], x_in.at[i, n], device))
-        flight.append(copies)
+        for dx in (2, 1, 3):
+            paired[i, dx] = add(block_of(at.slot(order[i], dx)), pair_in[i, dx])
+        if i > 0:
+            for copy in flight[max(0, i - 2)]:
+                copy.left()
+        flight.append(
+            [
+                wire.go(paired.at[i, dx], x_in.at[i, n], device)
+                for dx, n, device in ((2, 2, far), (1, 0, up), (3, 1, down))
+            ]
+        )
 
     def third(i):
         value = block_of(at.slot(order[i], 0)) + pair_in[i, 0].astype(F32)
@@ -328,12 +353,22 @@
         z_out[way, half, step] = (total[i, cut[half]] + z_in[way, half, step - 1].astype(F32)).astype(BF16)
         send(way, half, step)
 
+    cross(0)
+    cross(1)
+    first(0)
+    cross(2)
+    cross(3)
+    first(1)
+    first(2)
     third(0)
     start(0, 0, 0, 0)
     start(0, 1, 1, 0)
     third(1)
+    moving[0, 0].left()
     start(1, 0, 1, 1)
+    first(3)
     third(2)
+    moving[1, 1].left()
     start(2, 1, 0, 1)
     third(3)
     carry(1, 0, 0, 1)
@@ -373,8 +408,8 @@
         return block.at[at.slot(dh, 0), part[half]]
 
     moving = {}
-    for way, half in ((0, 0), (1, 1), (0, 1), (1, 0)):
-        moving[way, half] = wire.go(own.at[part[half]], place(0, half), along[way])
+    for way in (0, 1):
+        moving[way, way] = wire.go(own.at[part[way]], place(0, way), along[way])
     block[at.slot(0, 0)] = own[...]
 
     def spread(dh, half):
@@ -401,6 +436,9 @@
     here = [spread(0, half) for half in (0, 1)]
     for item in here:
         across(item)
+    for way in (0, 1):
+        moving[way, way].left()
+        moving[way, 1 - way] = wire.go(own.at[part[1 - way]], place(0, 1 - way), along[way])
     early = [arrive(0, 0, -1), arrive(1, 1, 1)]
     late = [arrive(0, 1, -1), arrive(1, 0, 1)]
     for item in early:

time: 152 us -> 150 us (0.987)
  the two profiles are of different devices: /device:TPU:1 before, /device:TPU:6 now
where the time goes in v3:
time: 150 us
  Pallas kernels  146 us (97%)
  local copies, waits for them, and re-layouts  2.14 us (1%)
    pallas_call x1, Pallas kernels, layer(): pl.pallas_call(k_layer, out_shape=(block, block), in_specs=[SMEM_SPEC] *...  145 us

profile of v3, /device:TPU:6, one launch (start us, length us, event | category | flops | bytes accessed | tf_op | source)
XLA Modules:
  0.0 149.9 jit_solution(17339146687242068153)
XLA Ops:
  1.3 1.9 %plan.1 = (s32[24]{0:T(128)}, s32[24]{0:T(128)}, s32[32]{0:T(128)}, s32[24]{0:T(128)}, s32[32]{0:T(128)}) custom-call(s32[24]{0:T(128)} %bitcast.8, s32[24]{0:T(128)} %bitcast.6, s32[1]{0:T(128)} %bitcast.4.count), custom_call_target="tpu_custom_call" | custom-call | tf_op jit(solution)/shard_map/plan/pallas_call | solution.py:521
  3.2 144.6 %layer.1 = (bf16[128,256]{1,0:T(8,128)(2,1)}, bf16[128,256]{1,0:T(8,128)(2,1)}) custom-call(s32[24]{0:T(128)} %bitcast.7, s32[24]{0:T(128)} %get-tuple-element.7.row_slot, s32[24]{0:T(128)} %get-tuple-element.8.row_before, s32[32]{0:T(128)} %get-tuple-element.9.row_last, s32[24]{0:T(128)} %get-tuple-element.10.col_before, s32[32]{0:T(128)} %get-tuple-element.11.col_last, ...), custom_call_target="tpu_custom_call" | custom-call | tf_op jit(solution)/shard_map/layer/pallas_call | solution.py:560
  147.8 0.0 copy-start
  147.8 1.5 %copy.12 = bf16[128,256]{1,0:T(8,128)(2,1)} copy(bf16[128,256]{1,0:T(8,128)(2,1)} %get-tuple-element.14) | data formatting | bytes 131072
  149.3 0.0 copy-done
  149.3 0.6 copy.13
Async XLA Ops:
  147.8 1.5 %copy-start = (bf16[128,256]{1,0:T(8,128)(2,1)S(1)}, bf16[128,256]{1,0:T(8,128)(2,1)}, u32[]{:S(2)}) copy-start(bf16[128,256]{1,0:T(8,128)(2,1)} %get-tuple-element.15) | copy-start | bytes 196612

commit v4 on v3

--- a/solution.py
+++ b/solution.py
@@ -111,7 +111,7 @@
 GATHER_ROW_COPIES = 14 + 5 * 6 + 3 * 6
 
 
-def gather_row(wire, at, own, block):
+def gather_row(wire, at, own, block, meanwhile):
     part = halves(own.shape[0])
     along = (at.row_device(1, 0), at.row_device(-1, 0))
     up, down, far = at.row_device(0, 1), at.row_device(0, -1), at.row_device(0, 2)
@@ -147,6 +147,7 @@
             moving[way, now] = wire.go(own.at[part[now]], place(0, 0, now), along[way])
     spreading = [spread(0, half, own.at[part[half]], False) for half in (0, 1)]
     block[at.row_of(0, 0)] = own[...]
+    meanwhile()
     for s in (1, 2, 3, 4):
         now = []
         for half in (0, 1):
@@ -474,7 +475,7 @@
             k = g * group + n
             product = lax.dot_general(
                 tiles[k],
-                source[source_at[k]],
+                source[source_at(k)],
                 (((contract,), (0,)), ((), ())),
                 preferred_element_type=F32,
             )
@@ -484,28 +485,28 @@
     lax.fori_loop(0, slots // group, some, 0)
 
 
-def k_plan(rows, cols, count, row_slot, row_before, row_last, col_before, col_last):
-    slots = rows.shape[0]
-
-    def clear(t, carry):
-        row_last[t] = jnp.int32(slots)
-        col_last[t] = jnp.int32(slots)
+def slot_tables(targets, count, before, last, target_at):
+    slots = targets.shape[0]
+    empty = jnp.int32(slots)
+    held = [jnp.where(n < count, targets[n], jnp.int32(-1)) for n in range(slots)]
+
+    def one_slot(k, carry):
+        own, found = targets[k], empty
+        for n in range(slots):
+            found = jnp.where((n < k) & (held[n] == own), jnp.int32(n), found)
+        before[k] = found
         return carry
 
-    lax.fori_loop(0, ROWS, clear, 0)
-
-    def slot(k, carry):
-        r, c = rows[k], cols[k]
-        s = rem(r, 2) * (NH * NX) + div(r, 2)
-        row_slot[k] = s
-        live = k < count[0]
-        old_row, old_col = row_last[s], col_last[c]
-        row_before[k], col_before[k] = old_row, old_col
-        row_last[s] = jnp.where(live, k, old_row)
-        col_last[c] = jnp.where(live, k, old_col)
+    def one_target(t, carry):
+        found = empty
+        own = target_at(t)
+        for n in range(slots):
+            found = jnp.where(held[n] == own, jnp.int32(n), found)
+        last[t] = found
         return carry
 
-    lax.fori_loop(0, slots, slot, 0)
+    lax.fori_loop(0, slots, one_slot, 0)
+    lax.fori_loop(0, last.shape[0], one_target, 0)
 
 
 SMEM_SPEC = pl.BlockSpec(memory_space=pltpu.SMEM)
@@ -514,24 +515,11 @@
 LIMIT = 56 * 1024 * 1024
 
 
-def plan(rows, cols, count):
-    slots = rows.shape[0]
-    one = jax.ShapeDtypeStruct((slots,), jnp.int32)
-    table = jax.ShapeDtypeStruct((ROWS,), jnp.int32)
-    return pl.pallas_call(
-        k_plan,
-        out_shape=(one, one, table, one, table),
-        in_specs=[SMEM_SPEC] * 3,
-        out_specs=(SMEM_SPEC,) * 5,
-        name="plan",
-    )(rows, cols, count)
-
-
 def k_layer(
-    col_at, row_slot, row_before, row_last, col_before, col_last,
-    own, tiles_hbm, weight, out_grad, layer_out, grad_x, *scratch
+    row_at, col_at, count, own, tiles_hbm, weight, out_grad, layer_out, grad_x, *scratch
 ):
     tiles, tile_sem, source, grads, projected, sums, *scratch = scratch
+    row_before, row_last, col_before, col_last, *scratch = scratch
     n_row, n_col = len(sum_row_scratch(32, 128)), len(sum_col_scratch(32, 128))
     row_buffers, col_buffers = scratch[:n_row], scratch[n_row : n_row + n_col]
     send, recv = scratch[n_row + n_col :]
@@ -541,18 +529,23 @@
     sums[tiles.shape[0]] = jnp.zeros(sums.shape[1:], F32)
     greet(at.row_neighbours() + at.col_neighbours())
     wire = Wire(send, recv)
-    gather_row(wire, at, own, source)
+
+    def tables():
+        slot_tables(row_at, count[0], row_before, row_last, lambda t: rem(t, NH * NX) * 2 + div(t, NH * NX))
+        slot_tables(col_at, count[0], col_before, col_last, lambda t: t)
+
+    gather_row(wire, at, own, source, tables)
     load.wait()
-    tile_sums(1, tiles, source, col_at, row_before, sums)
+    tile_sums(1, tiles, source, lambda k: col_at[k], row_before, sums)
     aggregated = sum_col(wire, at, lambda slot: sums[row_last[slot]], *col_buffers)
     projected[...] = dense(aggregated.astype(BF16), weight, out_grad, layer_out)
     gather_col(wire, at, projected, grads)
-    tile_sums(0, tiles, grads, row_slot, col_before, sums)
+    tile_sums(0, tiles, grads, lambda k: rem(row_at[k], 2) * (NH * NX) + div(row_at[k], 2), col_before, sums)
     sum_row(wire, at, lambda row: sums[col_last[row]], grad_x, *row_buffers)
     wire.drain()
 
 
-def layer(tables, own, tiles, weight, out_grad):
+def layer(rows_at, cols_at, count, own, tiles, weight, out_grad):
     rows, width = own.shape
     slots = tiles.shape[0]
     block = jax.ShapeDtypeStruct((rows, width), BF16)
@@ -560,7 +553,7 @@
     return pl.pallas_call(
         k_layer,
         out_shape=(block, block),
-        in_specs=[SMEM_SPEC] * 6 + [VMEM_SPEC, ANY_SPEC, VMEM_SPEC, VMEM_SPEC],
+        in_specs=[SMEM_SPEC] * 3 + [VMEM_SPEC, ANY_SPEC, VMEM_SPEC, VMEM_SPEC],
         out_specs=(VMEM_SPEC, VMEM_SPEC),
         scratch_shapes=[
             pltpu.VMEM(tiles.shape, BF16),
@@ -569,6 +562,10 @@
             pltpu.VMEM((COLS, rows, width), BF16),
             pltpu.VMEM((rows, width), BF16),
             pltpu.VMEM((slots + 1, rows, width), F32),
+            pltpu.SMEM((slots,), jnp.int32),
+            pltpu.SMEM((COLS,), jnp.int32),
+            pltpu.SMEM((slots,), jnp.int32),
+            pltpu.SMEM((ROWS,), jnp.int32),
         ]
         + sum_row_scratch(rows, width)
         + sum_col_scratch(rows, width)
@@ -577,13 +574,12 @@
             collective_id=0, has_side_effects=True, vmem_limit_bytes=LIMIT
         ),
         name="layer",
-    )(*tables, own, tiles, weight, out_grad)
+    )(rows_at, cols_at, count, own, tiles, weight, out_grad)
 
 
 def per_device(features, tile_values, tile_rows, tile_cols, tile_count, weight, out_grad):
     rows, cols = tile_rows[0, 0], tile_cols[0, 0]
-    tables = plan(rows, cols, tile_count[0])
-    return layer((cols,) + tuple(tables), features, tile_values[0, 0], weight, out_grad)
+    return layer(rows, cols, tile_count[0], features, tile_values[0, 0], weight, out_grad)
 
 
 def solution(mesh):

time: 150 us -> 148 us (0.987)
  Pallas kernels: 146 us -> 144 us
    pallas_call x1 -> x0, Pallas kernels: 1.87 us -> none  [plan(): pl.pallas_call(k_plan, out_shape=(one, one, table, one, table), in_specs=...]
where the time goes in v4:
time: 148 us
  Pallas kernels  144 us (97%)
  local copies, waits for them, and re-layouts  2.14 us (1%)
    pallas_call x1, Pallas kernels, layer(): pl.pallas_call(k_layer, out_shape=(block, block), in_specs=[SMEM_SPEC] *...  144 us

profile of v4, /device:TPU:6, one launch (start us, length us, event | category | flops | bytes accessed | tf_op | source)
XLA Modules:
  0.0 147.6 jit_solution(6480091745939398045)
XLA Ops:
  1.3 144.1 %layer.1 = (bf16[128,256]{1,0:T(8,128)(2,1)}, bf16[128,256]{1,0:T(8,128)(2,1)}) custom-call(s32[24]{0:T(128)} %bitcast.6, s32[24]{0:T(128)} %bitcast.7, s32[1]{0:T(128)} %bitcast.4.count, bf16[128,256]{1,0:T(8,128)(2,1)} %own.1, bf16[24,128,128]{2,1,0:T(8,128)(2,1)} %bitcast.5, bf16[256,256]{1,0:T(8,128)(2,1)} %weight.1, bf16[128,256]{1,0:T(8,128)(2,1)} %out_grad.1), custom_call_target="tpu_custom_call" | custom-call | tf_op jit(solution)/shard_map/layer/pallas_call | solution.py:553
  145.4 0.0 copy-start
  145.4 1.5 %copy.12 = bf16[128,256]{1,0:T(8,128)(2,1)} copy(bf16[128,256]{1,0:T(8,128)(2,1)} %get-tuple-element.4) | data formatting | bytes 131072
  146.9 0.0 copy-done
  146.9 0.6 copy.13
Async XLA Ops:
  145.4 1.5 %copy-start = (bf16[128,256]{1,0:T(8,128)(2,1)S(1)}, bf16[128,256]{1,0:T(8,128)(2,1)}, u32[]{:S(2)}) copy-start(bf16[128,256]{1,0:T(8,128)(2,1)} %get-tuple-element.5) | copy-start | bytes 196612

commit v5 on v4

--- a/solution.py
+++ b/solution.py
@@ -99,8 +99,8 @@
         self.started.append(Copy(copy))
         return self.started[-1]
 
-    def drain(self):
-        for copy in self.started:
+    def drain(self, until=None):
+        for copy in self.started[:until]:
             copy.left()
 
 
@@ -245,8 +245,10 @@
         z_out[way, half, step] = (total[i, cut[half]] + z_in[way, half, step - 1].astype(F32)).astype(BF16)
         send(way, half, step)
 
+    before = len(wire.started)
     for i in range(3):
         first(i)
+    wire.drain(before)
     third(0)
     start(0, 0, 0, 0)
     start(0, 1, 1, 0)
@@ -408,6 +410,7 @@
     def place(dh, half):
         return block.at[at.slot(dh, 0), part[half]]
 
+    before = len(wire.started)
     moving = {}
     for way in (0, 1):
         moving[way, way] = wire.go(own.at[part[way]], place(0, way), along[way])
@@ -435,6 +438,7 @@
         return spread(dh, half)
 
     here = [spread(0, half) for half in (0, 1)]
+    wire.drain(before)
     for item in here:
         across(item)
     for way in (0, 1):

time: 148 us -> 148 us (level)
  no operation moved by 1% of the time
where the time goes in v5:
time: 148 us; the launch traced here: 147 us
  Pallas kernels  144 us (97%)
  local copies, waits for them, and re-layouts  2.14 us (1%)
    pallas_call x1, Pallas kernels, layer(): pl.pallas_call(k_layer, out_shape=(block, block), in_specs=[SMEM_SPEC] *...  144 us

profile of v5, /device:TPU:6, one launch (start us, length us, event | category | flops | bytes accessed | tf_op | source)
XLA Modules:
  0.0 147.4 jit_solution(12055327230246925574)
XLA Ops:
  1.3 144.0 %layer.1 = (bf16[128,256]{1,0:T(8,128)(2,1)}, bf16[128,256]{1,0:T(8,128)(2,1)}) custom-call(s32[24]{0:T(128)} %bitcast.6, s32[24]{0:T(128)} %bitcast.7, s32[1]{0:T(128)} %bitcast.4.count, bf16[128,256]{1,0:T(8,128)(2,1)} %own.1, bf16[24,128,128]{2,1,0:T(8,128)(2,1)} %bitcast.5, bf16[256,256]{1,0:T(8,128)(2,1)} %weight.1, bf16[128,256]{1,0:T(8,128)(2,1)} %out_grad.1), custom_call_target="tpu_custom_call" | custom-call | tf_op jit(solution)/shard_map/layer/pallas_call | solution.py:557
  145.2 0.0 copy-start
  145.2 1.5 %copy.12 = bf16[128,256]{1,0:T(8,128)(2,1)} copy(bf16[128,256]{1,0:T(8,128)(2,1)} %get-tuple-element.4) | data formatting | bytes 131072
  146.8 0.0 copy-done
  146.8 0.6 copy.13
Async XLA Ops:
  145.2 1.5 %copy-start = (bf16[128,256]{1,0:T(8,128)(2,1)S(1)}, bf16[128,256]{1,0:T(8,128)(2,1)}, u32[]{:S(2)}) copy-start(bf16[128,256]{1,0:T(8,128)(2,1)} %get-tuple-element.5) | copy-start | bytes 196612
